TPU v7x, 256 devices: a whole 4x4x8 slice. The times are simulated.
256 devices in a mesh: dp: 4 (over y), seq: 64 (over z, x, core).
Axes of the slice: x: 4, y: 4, z: 8, core: 2. Of those that a mesh axis runs over, the one named last changes fastest.
Arguments:
- lin_q: bfloat16 [16384, 4096], P(('dp', 'seq')), parts along dimension 0, may hold values from -6 to 6
- lin_k: bfloat16 [16384, 4096], P(('dp', 'seq')), parts along dimension 0, may hold values from -0.59765625 to 0.59765625
- lin_v: bfloat16 [16384, 4096], P(('dp', 'seq')), parts along dimension 0, may hold values from -6 to 6
- log_decay: float32 [16384, 32], P(('dp', 'seq')), parts along dimension 0, may hold values from -1 to 0, as said below
- norm_gain: float32 [4096], replicated, may hold values from 0.1 to 1.9
- soft_q: bfloat16 [16384, 4096], P(('dp', 'seq')), parts along dimension 0, may hold values from -200 to 200
- soft_k: bfloat16 [16384, 512], P(('dp', 'seq')), parts along dimension 0, may hold values from -6 to 6
- soft_v: bfloat16 [16384, 512], P(('dp', 'seq')), parts along dimension 0, may hold values from -6 to 6
Outputs:
- lin_out: bfloat16 [16384, 4096], P(('dp', 'seq')), parts along dimension 0
- soft_out: bfloat16 [16384, 4096], P(('dp', 'seq')), parts along dimension 0
There are 4 independent parts, one for each index of `dp`. A program takes and returns all parts, laid end to end along the dimension named above; an argument that names none is the same for every part. Nothing has to cross between parts.
Inputs may be any that keep to these rules, and one draw needn't show every extreme that they name: `log_decay`: non-positive logarithms of decay factors.
All inputs are finite; a program needn't handle non-finite values.
Results may differ from a plain program's by a relative error of at most 0.01195.
Values may be sent and summed in bfloat16 or wider, within the bound.
No kernel may reach another device: no remote copies, remote signals or barrier semaphores. Data moves between devices by JAX's collectives and lax.ppermute only.
A program may use at most 384 MiB of HBM per device.

v0:
```python
import jax
import jax.numpy as jnp
from jax import lax
from jax.sharding import PartitionSpec as P


def entering(part, axis, combine, identity):
    place = lax.axis_index(axis)
    gathered = jax.tree.map(lambda a: lax.all_gather(a, axis), part)
    state = jax.tree.map(lambda a, e: jnp.zeros_like(a) + jnp.asarray(e, a.dtype), part, identity)

    def one(turn, state):
        return combine(
            state, jax.tree.map(lambda a: lax.dynamic_index_in_dim(a, turn, 0, False), gathered)
        )

    return lax.fori_loop(0, place, one, state)


def chain_combine(earlier, later):
    return (earlier[0] * later[0], later[0][:, None, None] * earlier[1] + later[1])


def on_device(lin_q, lin_k, lin_v, log_decay, norm_gain, soft_q, soft_k, soft_v):
    rows = lin_q.shape[0]
    heads = log_decay.shape[1]
    size = lin_q.shape[1] // heads
    q3 = lin_q.reshape(rows, heads, size)
    k3 = lin_k.reshape(rows, heads, size)
    v3 = lin_v.reshape(rows, heads, size)
    cum = jnp.cumsum(log_decay, axis=0)
    last = cum[-1]
    kw = k3.astype(jnp.float32) * jnp.exp(last[None, :] - cum)[:, :, None]
    contrib = jnp.einsum(
        "thd,the->hde", kw, v3.astype(jnp.float32), precision=lax.Precision.HIGHEST
    )
    index = lax.axis_index("seq")
    identity = (jnp.ones((heads,), jnp.float32), jnp.zeros((heads, size, size), jnp.float32))
    carried = entering((jnp.exp(last), contrib), "seq", chain_combine, identity)
    state_in = carried[1]
    scores = jnp.einsum("thd,shd->hts", q3, k3, preferred_element_type=jnp.float32)
    diff = cum.T[:, :, None] - cum.T[:, None, :]
    causal = jnp.arange(rows)[:, None] >= jnp.arange(rows)[None, :]
    weights = jnp.where(causal[None], jnp.exp(jnp.where(causal[None], diff, 0.0)), 0.0)
    intra_w = (scores * weights).astype(jnp.bfloat16)
    intra = jnp.einsum("hts,shd->thd", intra_w, v3, preferred_element_type=jnp.float32)
    qdec = q3.astype(jnp.float32) * jnp.exp(cum)[:, :, None]
    cross = jnp.einsum("thd,hde->the", qdec, state_in, precision=lax.Precision.HIGHEST)
    total = (intra + cross).reshape(rows, heads * size)
    rms = jnp.sqrt(jnp.mean(total * total, axis=1, keepdims=True) + 1e-06)
    lin_out = (total / rms * norm_gain[None, :]).astype(jnp.bfloat16)
    kv_heads = soft_k.shape[1] // size
    q_heads = soft_q.shape[1] // size
    group = q_heads // kv_heads
    positions = index * rows + jnp.arange(rows)
    top_pos = jnp.max(positions)
    q4 = soft_q.reshape(rows, kv_heads, group, size)
    scale = 1.0 / jnp.sqrt(jnp.float32(size))
    init = (
        jnp.full((rows, kv_heads, group), -1e30, jnp.float32),
        jnp.zeros((rows, kv_heads, group), jnp.float32),
        jnp.zeros((rows, kv_heads, group, size), jnp.float32),
    )
    key_piece = lax.all_gather(soft_k, "seq", axis=0, tiled=True)
    value_piece = lax.all_gather(soft_v, "seq", axis=0, tiled=True)
    count_rows = key_piece.shape[0]

    def compute(state):
        run_max, run_sum, accum = state
        k4 = key_piece.reshape(count_rows, kv_heads, size)
        v4 = value_piece.reshape(count_rows, kv_heads, size)
        s = jnp.einsum("tkge,nke->tkgn", q4, k4, preferred_element_type=jnp.float32) * scale
        key_pos = jnp.arange(count_rows)
        mask = (key_pos[None, :] <= positions[:, None])[:, None, None, :]
        s = jnp.where(mask, s, jnp.float32(-1e30))
        new_max = jnp.maximum(run_max, jnp.max(s, axis=3))
        probs = jnp.where(mask, jnp.exp(s - new_max[..., None]), 0.0)
        new_sum = jnp.sum(probs, axis=3)
        values = jnp.einsum(
            "tkgn,nke->tkge", probs.astype(jnp.bfloat16), v4, preferred_element_type=jnp.float32
        )
        return (new_max, new_sum, values)

    run_max, run_sum, accum = lax.cond(jnp.int32(0) <= top_pos, compute, lambda state: state, init)
    result = (accum / run_sum[..., None]).reshape(rows, q_heads * size).astype(jnp.bfloat16)
    return (lin_out, result)


def solution(mesh):
    in_specs = (
        P(("dp", "seq"), None),
        P(("dp", "seq"), None),
        P(("dp", "seq"), None),
        P(("dp", "seq"), None),
        P(),
        P(("dp", "seq"), None),
        P(("dp", "seq"), None),
        P(("dp", "seq"), None),
    )
    out_specs = (P(("dp", "seq"), None), P(("dp", "seq"), None))
    return jax.shard_map(
        on_device, mesh=mesh, in_specs=in_specs, out_specs=out_specs, check_vma=False
    )
```

profile of v0, /device:TPU:231, one launch (start us, length us, event | category | flops | bytes accessed | tf_op | source)
XLA Modules:
  0.0 741.6 jit_solution(1943864211326837046)
XLA Ops:
  9.7 4.5 fusion.24
  15.7 36.7 %all-gather.1 = f32[64,1,32]{2,1,0:T(1,128)S(1)} all-gather(f32[1,1,32]{2,1,0:T(1,128)S(1)} %get-tuple-element.81), channel_id=1, replica_groups=mesh['dp'=4,'seq'=64] {'seq'}, dimensions={0}, use_global_device_ids=true | all-gather | bytes 8320 | tf_op jit(solution)/shard_map/all_gather | solution.py:9
  52.4 2.8 convolution_bitcast_fusion.1
  55.2 32.3 %all-gather.6.cloned.1.call-done = bf16[4096,512]{1,0:T(8,128)(2,1)} async-done(((bf16[64,512]{1,0:T(8,128)(2,1)}), bf16[4096,512]{1,0:T(8,128)(2,1)}) %all-gather.6.cloned.1.call-update) | async-done | bytes 4194320 | tf_op jit(solution)/shard_map/all_gather | solution.py:64
  87.5 79.1 %all-gather.8.cloned.1.call-done = bf16[4096,512]{1,0:T(8,128)(2,1)} async-done(((bf16[64,512]{1,0:T(8,128)(2,1)}), bf16[4096,512]{1,0:T(8,128)(2,1)}) %all-gather.8.cloned.1.call-update) | async-done | bytes 4194320 | tf_op jit(solution)/shard_map/all_gather | solution.py:65
  166.6 67.4 %conditional.1 = (f32[64,4,8]{0,2,1:T(8,128)S(1)}, f32[64,4,8,128]{3,0,2,1:T(8,128)S(1)}) conditional(s32[]{:T(128)} %convert_element_type.29, () %tuple.24, (s32[64]{0:T(128)S(1)}, bf16[4096,512]{1,0:T(8,128)(2,1)}, bf16[64,4096]{1,0:T(8,128)(2,1)}, bf16[4096,512]{1,0:T(8,128)(2,1)}) %tuple.25), branch_computations={%region_5.6_spmd, %region_6.9_spmd} | conditional | flops 4404279296 | bytes 129548560 | solution.py:84
  166.8 6.9 reshape.87
  174.8 19.1 %fusion = (f32[64,4,8]{0,2,1:T(8,128)S(1)}, f32[4,4096,64,8]{1,2,3,0:T(8,128)}) fusion(pred[64,4096]{1,0:T(8,128)(4,1)S(1)} %iota_compare_fusion, bf16[64,4,8,128]{3,2,1,0:T(8,128)(2,1)S(1)} %bitcast.104, bf16[4096,4,128,1]{2,1,0,3:T(4,128)(2,1)} %bitcast.102), kind=kOutput, calls=%fused_computation.4 | convolution fusion | flops 2172647424 | bytes 38543360 | tf_op jit(solution)/shard_map/cond/branch_1_fun/tkge,nke->tkgn/dot_general | solution.py:72
  193.9 6.9 reshape.89
  200.9 16.9 %fusion.9 = f32[64,4,8,128]{3,0,2,1:T(8,128)S(1)} fusion(bf16[4096,4,128,1]{2,1,0,3:T(4,128)(2,1)} %bitcast.103, f32[4,4096,64,8]{1,2,3,0:T(8,128)} %get-tuple-element.77, f32[64,4,8]{0,2,1:T(8,128)S(1)} %broadcast_maximum_fusion, pred[64,4096]{1,0:T(8,128)(4,1)S(1)} %iota_compare_fusion), kind=kOutput, calls=%fused_computation.12 | convolution fusion | flops 2189426688 | bytes 39067648 | tf_op jit(solution)/shard_map/cond/branch_1_fun/tkgn,nke->tkge/dot_general | solution.py:79
  217.8 16.2 %fusion.2 = f32[64,4,8]{0,2,1:T(8,128)S(1)} fusion(f32[4,4096,64,8]{1,2,3,0:T(8,128)} %get-tuple-element.77, f32[64,4,8]{0,2,1:T(8,128)S(1)} %broadcast_maximum_fusion, pred[64,4096]{1,0:T(8,128)(4,1)S(1)} %iota_compare_fusion), kind=kLoop, calls=%fused_computation.6 | loop fusion | flops 41940992 | bytes 33832960 | tf_op jit(solution)/shard_map/cond/branch_1_fun/reduce_sum | solution.py:78
  235.7 366.9 %all-gather.10.cloned.1.call-done = f32[2048,128,128]{2,1,0:T(8,128)} async-done(((f32[32,128,128]{2,1,0:T(8,128)}), f32[2048,128,128]{2,1,0:T(8,128)}) %all-gather.10.cloned.1.call-update) | async-done | bytes 134217744 | tf_op jit(solution)/shard_map/all_gather | solution.py:9
  602.9 127.8 %while.12 = (s32[]{:T(128)}, f32[32,128,128]{2,1,0:T(8,128)S(1)}, s32[]{:T(128)}, f32[64,32]{1,0:T(8,128)S(1)}, f32[64,32,128,128]{3,2,1,0:T(8,128)}, /*index=5*/s32[]{:T(128)}, s32[]{:T(128)}, s32[]{:T(128)}) while((s32[]{:T(128)}, f32[32,128,128]{2,1,0:T(8,128)S(1)}, s32[]{:T(128)}, f32[64,32]{1,0:T(8,128)S(1)}, ...), condition=%wide.region_2.3_spmd, body=%wide.region_1.2_spmd.sunk | while | flops 1048581 | bytes 6291967 | solution.py:17
  603.1 2.0 bitcast_add_fusion.2
  605.1 2.0 bitcast_add_fusion.2
  607.2 2.0 bitcast_add_fusion.2
  609.2 2.0 bitcast_add_fusion.2
  611.2 2.0 bitcast_add_fusion.2
  613.2 2.0 bitcast_add_fusion.2
  615.3 2.0 bitcast_add_fusion.2
  617.3 2.0 bitcast_add_fusion.2
  623.4 2.0 bitcast_add_fusion.2
  625.4 2.0 bitcast_add_fusion.2
  627.4 2.0 bitcast_add_fusion.2
  637.5 2.0 bitcast_add_fusion.2
  639.6 2.0 bitcast_add_fusion.2
  641.6 2.0 bitcast_add_fusion.2
  649.7 2.0 bitcast_add_fusion.2
  651.7 2.0 bitcast_add_fusion.2
  653.7 2.0 bitcast_add_fusion.2
  661.8 2.0 bitcast_add_fusion.2
  663.9 2.0 bitcast_add_fusion.2
  665.9 2.0 bitcast_add_fusion.2
  676.0 2.0 bitcast_add_fusion.2
  678.0 2.0 bitcast_add_fusion.2
  680.1 2.0 bitcast_add_fusion.2
  688.2 2.0 bitcast_add_fusion.2
  690.2 2.0 bitcast_add_fusion.2
  692.2 2.0 bitcast_add_fusion.2
  700.3 2.0 bitcast_add_fusion.2
  702.4 2.0 bitcast_add_fusion.2
  704.4 2.0 bitcast_add_fusion.2
  714.5 2.0 bitcast_add_fusion.2
  716.5 2.0 bitcast_add_fusion.2
  718.6 2.0 bitcast_add_fusion.2
  726.7 2.0 bitcast_add_fusion.2
  728.7 2.0 bitcast_add_fusion.2
  730.7 3.4 multiply_reduce_fusion
  (123 shorter events, 65.5 us)
Async XLA Ops:
  7.2 2.5 copy-start
  7.2 80.3 %all-gather.6.cloned.1.call-start = ((), (), s32[]{:S(2)}) async-start(), calls=%async_computation | async-start | bytes 4259840 | tf_op jit(solution)/shard_map/all_gather | solution.py:64
  7.9 158.6 %all-gather.8.cloned.1.call-start = ((), (), s32[]{:S(2)}) async-start(), calls=%async_computation.1 | async-start | bytes 4259840 | tf_op jit(solution)/shard_map/all_gather | solution.py:65
  8.7 593.9 %all-gather.10.cloned.1.call-start = ((), (), s32[]{:S(2)}) async-start(), calls=%async_computation.2 | async-start | bytes 136314880 | tf_op jit(solution)/shard_map/all_gather | solution.py:9
  602.6 128.1 %copy-start.1 = (bf16[64,4096]{1,0:T(8,128)(2,1)S(1)}, bf16[64,4096]{1,0:T(8,128)(2,1)}, u32[]{:S(2)}) copy-start(bf16[64,4096]{1,0:T(8,128)(2,1)} %param.12) | copy-start | bytes 1572868
  602.8 131.2 %copy-start.2 = (f32[4096]{0:T(1024)S(1)}, f32[4096]{0:T(1024)}, u32[]{:S(2)}) copy-start(f32[4096]{0:T(1024)} %param.16) | copy-start | bytes 49156
Sparse Core Ops, SparseCore 0:
  10.8 76.6 all-gather.5
  90.3 76.2 all-gather.7
  169.3 433.2 all-gather.9
where the time goes:
time: 744 us; the launch traced here: 742 us
  waiting for transfers between devices  480 us (65%)
  other arithmetic  143 us (19%)
  matrix products  46.7 us (6%)
  blocking collectives  36.7 us (5%)
  local copies, waits for them, and re-layouts  18.2 us (2%)
  between operations  14.5 us (2%)
    all_gather x1, waiting for transfers between devices, entering(): gathered = jax.tree.map(lambda a: lax.all_gather(a, axis), part)  367 us
    add x63, other arithmetic, chain_combine(): later[0][:, None, None] * earlier[1] + later[1]  124 us
    all_gather x1, waiting for transfers between devices, on_device(): value_piece = lax.all_gather(soft_v, 'seq', axis=0, tiled=True)  79.1 us
    all_gather x1, blocking collectives, entering(): gathered = jax.tree.map(lambda a: lax.all_gather(a, axis), part)  36.7 us
    all_gather x1, waiting for transfers between devices, on_device(): key_piece = lax.all_gather(soft_k, 'seq', axis=0, tiled=True)  32.3 us
    dot_general x1, matrix products, compute(): jnp.einsum('tkge,nke->tkgn', q4, k4, preferred_element_type=jnp.float32)  19.1 us
    dot_general x1, matrix products, compute(): jnp.einsum('tkgn,nke->tkge', probs.astype(jnp.bfloat16), v4, preferred_el...  16.9 us
    reduce_sum x1, other arithmetic, compute(): new_sum = jnp.sum(probs, axis=3)  16.2 us
  transfers between devices with their start and end apart: 3, of which 3 were waited for; matrix products, arithmetic and copies ran while one was open for 11% of the time, Pallas kernels for 0%

commit v1 on v0

v1 whole, which is shorter than its diff:
```python
import functools

import jax
import jax.numpy as jnp
from jax import lax
from jax.experimental import pallas as pl
from jax.experimental.pallas import tpu as pltpu
from jax.sharding import PartitionSpec as P

SIZE = 128
F32 = jnp.float32
BF16 = jnp.bfloat16
VMEM_LIMIT = 48 * 1024 * 1024
EXTRA = 16


def params():
    return pltpu.CompilerParams(vmem_limit_bytes=VMEM_LIMIT)


def running_sum(log_decay):
    rows = log_decay.shape[0]
    t = lax.broadcasted_iota(jnp.int32, (rows, rows), 0)
    s = lax.broadcasted_iota(jnp.int32, (rows, rows), 1)
    lower = jnp.where(s <= t, 1.0, 0.0).astype(F32)
    return jnp.dot(lower, log_decay, precision=lax.Precision.HIGHEST, preferred_element_type=F32)


def running_sum_rows(log_decay):
    rows = log_decay.shape[0]
    s = lax.broadcasted_iota(jnp.int32, (rows, rows), 0)
    t = lax.broadcasted_iota(jnp.int32, (rows, rows), 1)
    upper = jnp.where(s <= t, 1.0, 0.0).astype(F32)
    return lax.dot_general(
        log_decay,
        upper,
        (((0,), (0,)), ((), ())),
        precision=lax.Precision.HIGHEST,
        preferred_element_type=F32,
    )


def contrib_kernel(k_ref, v_ref, decay_ref, out_ref):
    heads = decay_ref.shape[1]
    half = SIZE // 2
    cum = running_sum(decay_ref[...])
    last = cum[-1:, :]
    to_end = jnp.exp(last - cum)
    row = lax.broadcasted_iota(jnp.int32, (EXTRA, SIZE), 0)
    for h in range(heads):
        cols = slice(h * SIZE, (h + 1) * SIZE)
        kw = (k_ref[:, cols].astype(F32) * to_end[:, h : h + 1]).astype(BF16)
        state = lax.dot_general(
            kw, v_ref[:, cols], (((0,), (0,)), ((), ())), preferred_element_type=F32
        ).astype(BF16)
        total = jnp.broadcast_to(last[:, h : h + 1], (EXTRA, SIZE))
        high = total.astype(BF16).astype(F32)
        mid = (total - high).astype(BF16).astype(F32)
        low = total - high - mid
        terms = jnp.where(row == 0, high, jnp.where(row == 1, mid, jnp.where(row == 2, low, 0.0)))
        terms = terms.astype(BF16)
        for part in range(2):
            out_ref[2 * h + part, :half, :] = state[part * half : (part + 1) * half]
            out_ref[2 * h + part, half:, :] = terms


def contributions(k, v, log_decay):
    heads = log_decay.shape[1]
    return pl.pallas_call(
        contrib_kernel,
        out_shape=jax.ShapeDtypeStruct((2 * heads, SIZE // 2 + EXTRA, SIZE), BF16),
        compiler_params=params(),
    )(k, v, log_decay)


def scan_kernel(in_ref, out_ref):
    slabs = in_ref.shape[0]
    half = SIZE // 2

    def step(n, state):
        out_ref[n] = state.astype(BF16)
        terms = in_ref[n, half:, :].astype(F32)
        gain = jnp.exp(jnp.sum(terms, axis=0, keepdims=True))
        return state * gain + in_ref[n, :half, :].astype(F32)

    lax.fori_loop(0, slabs, step, jnp.zeros((half, SIZE), F32), unroll=4)


def scan_states(parts):
    return pl.pallas_call(
        scan_kernel,
        out_shape=jax.ShapeDtypeStruct((parts.shape[0], SIZE // 2, SIZE), BF16),
        compiler_params=params(),
    )(parts)


def intra_kernel(q_ref, k_ref, v_ref, decay_ref, out_ref):
    rows, heads = decay_ref.shape
    cum = running_sum(decay_ref[...])
    cum_rows = running_sum_rows(decay_ref[...])
    t = lax.broadcasted_iota(jnp.int32, (rows, rows), 0)
    s = lax.broadcasted_iota(jnp.int32, (rows, rows), 1)
    causal = s <= t
    for h in range(heads):
        cols = slice(h * SIZE, (h + 1) * SIZE)
        score = lax.dot_general(
            q_ref[:, cols], k_ref[:, cols], (((1,), (1,)), ((), ())), preferred_element_type=F32
        )
        diff = jnp.where(causal, cum[:, h : h + 1] - cum_rows[h : h + 1, :], 0.0)
        weight = jnp.where(causal, score * jnp.exp(diff), 0.0).astype(BF16)
        out_ref[:, cols] = jnp.dot(weight, v_ref[:, cols], preferred_element_type=F32)


def intra_part(q, k, v, log_decay):
    return pl.pallas_call(
        intra_kernel,
        out_shape=jax.ShapeDtypeStruct(q.shape, F32),
        compiler_params=params(),
    )(q, k, v, log_decay)


def final_kernel(q_ref, intra_ref, state_ref, decay_ref, gain_ref, out_ref, total_ref):
    rows, heads = decay_ref.shape
    grown = jnp.exp(running_sum(decay_ref[...]))
    square = jnp.zeros((rows, SIZE), F32)
    for h in range(heads):
        cols = slice(h * SIZE, (h + 1) * SIZE)
        cross = jnp.dot(q_ref[:, cols], state_ref[h], preferred_element_type=F32)
        total = intra_ref[:, cols] + grown[:, h : h + 1] * cross
        total_ref[:, cols] = total
        square += total * total
    mean = jnp.sum(square, axis=1, keepdims=True) / (heads * SIZE)
    scale = lax.rsqrt(mean + 1e-06)
    for h in range(heads):
        cols = slice(h * SIZE, (h + 1) * SIZE)
        out_ref[:, cols] = (total_ref[:, cols] * scale * gain_ref[:, cols]).astype(BF16)


def final_part(q, intra, state, log_decay, gain):
    return pl.pallas_call(
        final_kernel,
        out_shape=jax.ShapeDtypeStruct(q.shape, BF16),
        scratch_shapes=[pltpu.VMEM(q.shape, F32)],
        compiler_params=params(),
    )(q, intra, state, log_decay, gain)


LOG2E = 1.4426950408889634


def flash_kernel(block, base_ref, q_ref, k_ref, v_ref, out_ref, rows_ref):
    tokens = q_ref.shape[0]
    group = q_ref.shape[1] // SIZE
    base = base_ref[0]
    for h in range(group):
        rows_ref[h * tokens : (h + 1) * tokens, :] = q_ref[:, h * SIZE : (h + 1) * SIZE]
    q = rows_ref[...]
    width = group * tokens
    scale = LOG2E / (SIZE**0.5)

    def visit(start, carry, masked):
        top, norm, accum = carry
        k = k_ref[pl.ds(start, block), :]
        v = v_ref[pl.ds(start, block), :]
        s = lax.dot_general(k, q, (((1,), (1,)), ((), ())), preferred_element_type=F32) * scale
        if masked:
            key = start + lax.broadcasted_iota(jnp.int32, s.shape, 0)
            token = base + lax.rem(lax.broadcasted_iota(jnp.int32, s.shape, 1), tokens)
            s = jnp.where(key <= token, s, -1e30)
        new_top = jnp.maximum(top, jnp.max(s, axis=0, keepdims=True))
        shrink = jnp.exp2(top - new_top)
        p = jnp.exp2(s - new_top)
        norm = norm * shrink + jnp.sum(p, axis=0, keepdims=True)
        got = lax.dot_general(
            v, p.astype(BF16), (((0,), (0,)), ((), ())), preferred_element_type=F32
        )
        return new_top, norm, accum * shrink + got

    full = lax.div(base, block)
    carry = (
        jnp.full((1, width), -1e30, F32),
        jnp.zeros((1, width), F32),
        jnp.zeros((SIZE, width), F32),
    )
    carry = visit(pl.multiple_of(full * block, block), carry, True)
    top, norm, accum = lax.fori_loop(
        0, full, lambda i, c: visit(pl.multiple_of(i * block, block), c, False), carry
    )
    out = jnp.transpose(accum / norm).astype(BF16)
    for h in range(group):
        out_ref[:, h * SIZE : (h + 1) * SIZE] = out[h * tokens : (h + 1) * tokens]


def flash(q, kv, base, block=512):
    tokens = q.shape[0]
    kv_heads = kv.shape[1] // (2 * SIZE)
    width = q.shape[1] // kv_heads
    keys = kv.shape[0]
    return pl.pallas_call(
        functools.partial(flash_kernel, block),
        out_shape=jax.ShapeDtypeStruct(q.shape, BF16),
        grid_spec=pltpu.PrefetchScalarGridSpec(
            num_scalar_prefetch=1,
            grid=(kv_heads,),
            in_specs=[
                pl.BlockSpec((tokens, width), lambda g, b: (0, g)),
                pl.BlockSpec((keys, SIZE), lambda g, b: (0, g)),
                pl.BlockSpec((keys, SIZE), lambda g, b: (0, kv_heads + g)),
            ],
            out_specs=pl.BlockSpec((tokens, width), lambda g, b: (0, g)),
            scratch_shapes=[pltpu.VMEM((width // SIZE * tokens, SIZE), BF16)],
        ),
        compiler_params=params(),
    )(base, q, kv, kv)


def on_device(lin_q, lin_k, lin_v, log_decay, norm_gain, soft_q, soft_k, soft_v):
    tokens = lin_q.shape[0]
    heads = log_decay.shape[1]
    base = (lax.axis_index("seq") * tokens).astype(jnp.int32).reshape(1)
    with jax.named_scope("keys_values"):
        kv = lax.all_gather(jnp.concatenate([soft_k, soft_v], axis=1), "seq", axis=0, tiled=True)
    with jax.named_scope("states"):
        parts = contributions(lin_k, lin_v, log_decay)
        parts = lax.all_to_all(parts, "seq", 0, 0)
        intra = intra_part(lin_q, lin_k, lin_v, log_decay)
        states = scan_states(parts)
        states = lax.all_to_all(states, "seq", 0, 0).reshape(heads, SIZE, SIZE)
        lin_out = final_part(lin_q, intra, states, log_decay, norm_gain.reshape(1, -1))
    with jax.named_scope("softmax"):
        soft_out = flash(soft_q, kv, base)
    return lin_out, soft_out


def solution(mesh):
    split = P(("dp", "seq"), None)
    in_specs = (split,) * 4 + (P(),) + (split,) * 3
    return jax.shard_map(
        on_device, mesh=mesh, in_specs=in_specs, out_specs=(split, split), check_vma=False
    )
```

time: 744 us -> 148 us (0.20)
  waiting for transfers between devices: 480 us -> 40 us
  other arithmetic: 143 us -> 1.54 us
  matrix products: 46.7 us -> 0 us
  Pallas kernels: 0 us -> 33.7 us
  local copies, waits for them, and re-layouts: 18.2 us -> 3.93 us
  starting transfers between devices: 0.11 us -> 10.1 us
    all_gather x3 -> x1, waiting for transfers between devices: 478 us -> 9.72 us  [on_device(): lax.all_gather(jnp.concatenate([soft_k, soft_v], axis=1), 'seq', axis=0,...]
    add x64 -> x0, other arithmetic: 124 us -> none  [the longest x63 124 us: chain_combine(): later[0][:, None, None] * earlier[1] + later[1]]
    dot_general x5 -> x0, matrix products: 46.7 us -> none  [the longest x1 19.1 us: compute(): jnp.einsum('tkge,nke->tkgn', q4, k4, preferred_element_type=jnp.float32)]
    all_to_all x0 -> x1, blocking collectives: none -> 44.1 us  [on_device(): parts = lax.all_to_all(parts, 'seq', 0, 0)]
    all_gather x1 -> x0, blocking collectives: 36.7 us -> none  [entering(): gathered = jax.tree.map(lambda a: lax.all_gather(a, axis), part)]
    pallas_call x0 -> x5, Pallas kernels: none -> 33.7 us  [the longest x1 24.8 us: flash(): pl.pallas_call(functools.partial(flash_kernel, block), out_shape=jax.Shap...]
    all_to_all x0 -> x1, waiting for transfers between devices: none -> 30.3 us  [on_device(): states = lax.all_to_all(states, 'seq', 0, 0).reshape(heads, SIZE, SIZE)]
    reduce_sum x1 -> x0, other arithmetic: 16.2 us -> none  [compute(): new_sum = jnp.sum(probs, axis=3)]
  transfers between devices with their start and end apart: 3 -> 2, of which waited for: 3 -> 2; matrix products, arithmetic and copies ran while one was open for 11% -> 1% of each run, Pallas kernels for 0% -> 6%
where the time goes in v1:
time: 148 us; the launch traced here: 147 us
  blocking collectives  44.1 us (30%)
  waiting for transfers between devices  40 us (27%)
  Pallas kernels  33.7 us (23%)
  between operations  14.1 us (10%)
  starting transfers between devices  10.1 us (7%)
  local copies, waits for them, and re-layouts  3.93 us (3%)
  other arithmetic  1.54 us (1%)
    all_to_all x1, blocking collectives, on_device(): parts = lax.all_to_all(parts, 'seq', 0, 0)  44.1 us
    all_to_all x1, waiting for transfers between devices, on_device(): states = lax.all_to_all(states, 'seq', 0, 0).reshape(heads, SIZE, SIZE)  30.3 us
    pallas_call x1, Pallas kernels, flash(): pl.pallas_call(functools.partial(flash_kernel, block), out_shape=jax.Shap...  24.8 us
    all_to_all x1, starting transfers between devices, on_device(): states = lax.all_to_all(states, 'seq', 0, 0).reshape(heads, SIZE, SIZE)  10 us
    all_gather x1, waiting for transfers between devices, on_device(): lax.all_gather(jnp.concatenate([soft_k, soft_v], axis=1), 'seq', axis=0,...  9.72 us
    pallas_call x1, Pallas kernels, intra_part(): pl.pallas_call(intra_kernel, out_shape=jax.ShapeDtypeStruct(q.shape, F32)...  4.54 us
    unnamed x15, local copies, waits for them, and re-layouts  3.93 us
  transfers between devices with their start and end apart: 2, of which 2 were waited for; matrix products, arithmetic and copies ran while one was open for 1% of the time, Pallas kernels for 6%

profile of v1, /device:TPU:231, one launch (start us, length us, event | category | flops | bytes accessed | tf_op | source)
XLA Modules:
  0.0 147.5 jit_solution(9601078311352436625)
XLA Ops:
  7.2 0.0 all-gather.2.cloned.1.call-start
  7.2 1.5 %pad_maximum_fusion = bf16[64,1024]{1,0:T(8,128)(2,1)} fusion(bf16[64,512]{1,0:T(8,128)(2,1)} %param.15, bf16[64,512]{1,0:T(8,128)(2,1)} %param.14), kind=kLoop, calls=%fused_computation | loop fusion | flops 262144 | bytes 262144 | tf_op jit(solution)/shard_map/keys_values/concatenate | solution.py:222
  8.7 0.0 all-gather.2.cloned.1.call-update
  8.8 0.8 copy.10.decay_ref
  9.6 0.0 copy-start.1
  9.6 1.0 copy-done.1
  10.6 0.0 copy-start.3
  10.6 1.0 copy-done.3
  11.7 1.1 states.5
  12.8 44.1 %all_to_all.10.in_ref = bf16[64,80,128]{2,1,0:T(8,128)(2,1)S(1)} all-to-all(bf16[64,80,128]{2,1,0:T(8,128)(2,1)S(1)} %states.5), channel_id=1, replica_groups=mesh['dp'=4,'seq'=64] {'seq'}, dimensions={0} | all-to-all | bytes 2621440 | tf_op jit(solution)/shard_map/states/all_to_all | solution.py:225
  57.0 1.6 %states.6 = bf16[64,64,128]{2,1,0:T(8,128)(2,1)} custom-call(bf16[64,80,128]{2,1,0:T(8,128)(2,1)S(1)} %all_to_all.10.in_ref), custom_call_target="tpu_custom_call" | custom-call | tf_op jit(solution)/shard_map/states/pallas_call | solution.py:90
  58.5 0.0 copy-start
  58.5 0.0 copy-start.2
  58.5 10.0 %all-to-all-start.1 = ((bf16[64,64,128]{2,1,0:T(8,128)(2,1)}), bf16[64,64,128]{2,1,0:T(8,128)(2,1)S(1)}, u32[]{:S(2)}, u32[]{:S(2)}) async-start(bf16[64,64,128]{2,1,0:T(8,128)(2,1)} %states.6), calls=%async_computation.1 | async-start | bytes 2097152 | tf_op jit(solution)/shard_map/states/all_to_all | solution.py:228
  68.6 0.0 copy-done
  68.6 0.0 copy-done.2
  68.6 0.0 copy-start.4
  68.6 1.0 copy-done.4
  69.6 0.0 copy-start.6
  69.6 4.5 %states.4.intra_ref = f32[64,4096]{1,0:T(8,128)S(1)} custom-call(bf16[64,4096]{1,0:T(8,128)(2,1)S(1)} %copy-done, bf16[64,4096]{1,0:T(8,128)(2,1)S(1)} %copy-done.2, bf16[64,4096]{1,0:T(8,128)(2,1)S(1)} %copy-done.4, f32[64,32]{1,0:T(8,128)S(1)} %copy.10.decay_ref), custom_call_target="tpu_custom_call" | custom-call | tf_op jit(solution)/shard_map/states/pallas_call | solution.py:115
  74.2 30.3 %all-to-all-done.1 = bf16[64,64,128]{2,1,0:T(8,128)(2,1)S(1)} async-done(((bf16[64,64,128]{2,1,0:T(8,128)(2,1)}), bf16[64,64,128]{2,1,0:T(8,128)(2,1)S(1)}, u32[]{:S(2)}, u32[]{:S(2)}) %all-to-all-start.1) | async-done | bytes 1048608 | tf_op jit(solution)/shard_map/states/all_to_all | solution.py:228
  104.4 0.0 copy-done.6
  104.4 0.0 copy-start.5
  104.4 1.6 %states.7 = bf16[64,4096]{1,0:T(8,128)(2,1)} custom-call(bf16[64,4096]{1,0:T(8,128)(2,1)S(1)} %copy-done, f32[64,4096]{1,0:T(8,128)S(1)} %states.4.intra_ref, bf16[32,128,128]{2,1,0:T(8,128)(2,1)S(1)} %bitcast.3, f32[64,32]{1,0:T(8,128)S(1)} %copy.10.decay_ref, f32[1,4096]{1,0:T(1,128)S(1)} %bitcast.4), custom_call_target="tpu_custom_call" | custom-call | tf_op jit(solution)/shard_map/states/pallas_call | solution.py:140
  106.1 9.7 %all-gather.2.cloned.1.call-done.k_ref.v_ref = bf16[4096,1024]{1,0:T(8,128)(2,1)} async-done(((bf16[64,1024]{1,0:T(8,128)(2,1)}), bf16[4096,1024]{1,0:T(8,128)(2,1)}) %all-gather.2.cloned.1.call-update) | async-done | bytes 8388624 | tf_op jit(solution)/shard_map/keys_values/all_gather | solution.py:222
  115.8 0.0 copy-done.5
  115.8 24.8 %softmax.1 = bf16[64,4096]{1,0:T(8,128)(2,1)} custom-call(s32[1]{0:T(128)} %bitcast.2.base_ref, bf16[64,4096]{1,0:T(8,128)(2,1)S(1)} %copy-done.5, bf16[4096,1024]{1,0:T(8,128)(2,1)} %all-gather.2.cloned.1.call-done.k_ref.v_ref, bf16[4096,1024]{1,0:T(8,128)(2,1)} %all-gather.2.cloned.1.call-done.k_ref.v_ref), custom_call_target="tpu_custom_call" | custom-call | tf_op jit(solution)/shard_map/softmax/pallas_call | solution.py:199
Async XLA Ops:
  7.2 108.6 %all-gather.2.cloned.1.call-start = ((), (), s32[]{:S(2)}) async-start(), calls=%async_computation.2 | async-start | bytes 8519680 | tf_op jit(solution)/shard_map/keys_values/all_gather | solution.py:222
  9.6 1.0 copy-start.1
  10.6 1.0 copy-start.3
  58.5 10.0 %copy-start = (bf16[64,4096]{1,0:T(8,128)(2,1)S(1)}, bf16[64,4096]{1,0:T(8,128)(2,1)}, u32[]{:S(2)}) copy-start(bf16[64,4096]{1,0:T(8,128)(2,1)} %q_ref.4) | copy-start | bytes 1572868
  58.5 10.1 %copy-start.2 = (bf16[64,4096]{1,0:T(8,128)(2,1)S(1)}, bf16[64,4096]{1,0:T(8,128)(2,1)}, u32[]{:S(2)}) copy-start(bf16[64,4096]{1,0:T(8,128)(2,1)} %k_ref.3) | copy-start | bytes 1572868
  58.5 45.9 %all-to-all-start.1 = ((bf16[64,64,128]{2,1,0:T(8,128)(2,1)}), bf16[64,64,128]{2,1,0:T(8,128)(2,1)S(1)}, u32[]{:S(2)}, u32[]{:S(2)}) async-start(bf16[64,64,128]{2,1,0:T(8,128)(2,1)} %states.6), calls=%async_computation.1 | async-start | bytes 2097152 | tf_op jit(solution)/shard_map/states/all_to_all | solution.py:228
  68.6 1.0 copy-start.4
  69.6 34.8 %copy-start.6 = (f32[4096]{0:T(1024)S(1)}, f32[4096]{0:T(1024)}, u32[]{:S(2)}) copy-start(f32[4096]{0:T(1024)} %param.12) | copy-start | bytes 49156
  104.4 11.4 %copy-start.5 = (bf16[64,4096]{1,0:T(8,128)(2,1)S(1)}, bf16[64,4096]{1,0:T(8,128)(2,1)}, u32[]{:S(2)}) copy-start(bf16[64,4096]{1,0:T(8,128)(2,1)} %q_ref.5) | copy-start | bytes 1572868
Sparse Core Ops, SparseCore 0:
  11.3 104.4 all-gather.1
